TPU v7x, 128 devices: a whole 4x4x4 slice. The times are simulated.
128 devices in a mesh: inp: 8 (over x, y_lo), tm: 16 (over y_hi, z, core).
Axes of the slice: x: 4, y: 4 (y_hi: 2, y_lo: 2; y = y_hi * 2 + y_lo), z: 4, core: 2. Of those that a mesh axis runs over, the one named last changes fastest.
Arguments:
- samples: int32 [512, 524288], P('inp', 'tm'), may hold values from -8 to 7
- filter_taps: int32 [4, 2048], replicated, may hold values from -4096 to 4095
Outputs:
- visibilities: float32 [2, 1024, 512, 512], P(None, ('inp', 'tm'))
All inputs are finite; a program needn't handle non-finite values.
Results may differ from a plain program's by a relative error of at most 0.0032.
Values may be sent and summed in bfloat16 or wider, within the bound.
A program may use at most 128 MiB of HBM per device.

v0:
```python
import math

import jax
import jax.numpy as jnp
from jax import lax
from jax.sharding import PartitionSpec as P

BLOCKS = 4
SPEC_BLK = 4


def shifted(value, axis, steps):
    count = lax.axis_size(axis)
    initial, last = (max(0, -steps), min(count, count - steps))
    return lax.ppermute(value, axis, [(source, source + steps) for source in range(initial, last)])


def dft_table(frame_len, channels):
    points = lax.broadcasted_iota(jnp.int32, (channels, frame_len), 1)
    freqs = lax.broadcasted_iota(jnp.int32, (channels, frame_len), 0)
    angle = (points * freqs % frame_len).astype(jnp.float32) * (2.0 * math.pi / frame_len)
    scale = 1.0 / math.sqrt(frame_len)
    paired = jnp.stack([jnp.cos(angle) * scale, -jnp.sin(angle) * scale], axis=1)
    return paired.reshape(2 * channels, frame_len)


def on_device(samples, filter_taps):
    local_inputs = samples.shape[0]
    tap_count = filter_taps.shape[0]
    frame_len = filter_taps.shape[1]
    spec_dev = samples.shape[1] // frame_len
    channels = frame_len // 2
    inp_count = lax.axis_size("inp")
    tm_count = lax.axis_size("tm")
    all_inputs = local_inputs * inp_count
    chan_dev = channels // (inp_count * tm_count)
    total_spectra = spec_dev * tm_count
    row_width = 2 * SPEC_BLK * local_inputs
    frames = jnp.transpose(samples.reshape(local_inputs, spec_dev, frame_len), (1, 0, 2)).astype(
        jnp.bfloat16
    )
    history = shifted(frames[spec_dev - (tap_count - 1) :], "tm", 1)
    extended = jnp.concatenate([history, frames], axis=0)
    weights = filter_taps.astype(jnp.float32) / 16384.0
    table = dft_table(frame_len, channels)
    highest = lax.Precision.HIGHEST
    collected = []
    for block in range(BLOCKS):
        first = block * SPEC_BLK
        window = extended[first : first + SPEC_BLK + tap_count - 1].astype(jnp.float32)
        filtered = jnp.zeros((SPEC_BLK, local_inputs, frame_len), jnp.float32)
        for offset in range(tap_count):
            filtered = filtered + weights[offset] * window[offset : offset + SPEC_BLK]
        filtered = lax.optimization_barrier(filtered.astype(jnp.bfloat16)).astype(jnp.float32)
        filtered = filtered.reshape(SPEC_BLK * local_inputs, frame_len)
        spectra = lax.dot_general(table, filtered, (((1,), (1,)), ((), ())), precision=highest)
        spectra = spectra.reshape(channels, row_width)
        arrived = lax.all_to_all(
            lax.all_to_all(spectra, "inp", split_axis=0, concat_axis=1, tiled=True),
            "tm",
            split_axis=0,
            concat_axis=1,
            tiled=True,
        )
        collected.append(arrived.reshape(chan_dev, tm_count, inp_count, 2, SPEC_BLK, local_inputs))
    gathered = jnp.stack(collected, axis=1)
    ordered = jnp.transpose(gathered, (0, 4, 1, 2, 5, 3, 6))
    ordered = ordered.reshape(chan_dev, 2, BLOCKS * tm_count * SPEC_BLK, all_inputs)
    power = jnp.einsum("cpma,cpmb->cab", ordered, ordered, precision=highest)
    cross = jnp.einsum("cma,cmb->cab", ordered[:, 1], ordered[:, 0], precision=highest)
    phase = cross - jnp.transpose(cross, (0, 2, 1))
    return jnp.stack([power, phase]) / total_spectra


def solution(mesh):
    placed = (P("inp", "tm"), P())
    return jax.shard_map(
        on_device,
        mesh=mesh,
        in_specs=placed,
        out_specs=P(None, ("inp", "tm"), None, None),
        check_vma=False,
    )
```

profile of v0, /device:TPU:1, one launch (start us, length us, event | category | flops | bytes accessed | tf_op | source)
XLA Modules:
  0.0 527.6 jit_solution(10749850954218894469)
XLA Ops:
  12.4 34.9 %negate_multiply_fusion = (f32[1024,1,2048]{2,0,1:T(8,128)}, f32[1024,1,2048]{2,0,1:T(8,128)}) fusion(), kind=kLoop, calls=%fused_computation.11 | loop fusion | flops 35651584 | bytes 16777216 | tf_op jit(solution)/shard_map/mul | solution.py:23
  47.3 6.5 %pad_maximum_fusion = f32[1024,2,2048]{2,0,1:T(8,128)S(1)} fusion(f32[1024,1,2048]{2,0,1:T(8,128)} %get-tuple-element.16, f32[1024,1,2048]{2,0,1:T(8,128)} %get-tuple-element.17), kind=kLoop, calls=%fused_computation | loop fusion | flops 4194304 | bytes 33554432 | tf_op jit(solution)/shard_map/stack | solution.py:23
  53.8 21.3 %copy.70 = f32[1024,2,2048]{2,1,0:T(2,128)} copy(f32[1024,2,2048]{2,0,1:T(8,128)S(1)} %pad_maximum_fusion) | data formatting | bytes 33554432 | tf_op jit(solution)/shard_map/stack | solution.py:23
  75.2 20.5 %reshape.131 = f32[2048,2048]{1,0:T(8,128)} reshape(f32[1024,2,2048]{2,1,0:T(2,128)} %copy.70) | data formatting | bytes 33554432 | tf_op jit(solution)/shard_map/reshape | solution.py:24
  96.4 9.2 %fusion.24 = (f32[7,64,2048]{2,0,1:T(8,128)}, f32[7,64,2048]{2,0,1:T(8,128)S(1)}, f32[7,64,2048]{2,0,1:T(8,128)}, f32[7,64,2048]{2,0,1:T(8,128)}) fusion(bf16[16,64,2048]{2,0,1:T(8,128)(2,1)} %bitcast.53, bf16[3,64,2048]{2,0,1:T(4,128)(2,1)S(1)} %copy.72), kind=kLoop, calls=%fused_computation.56 | loop fusion | flops 6422528 | bytes 25952256 | tf_op jit(solution)/shard_map/convert_element_type | solution.py:50
  109.8 8.3 %fusion.29 = f32[2048,256]{1,0:T(8,128)S(1)} fusion(f32[2048,2048]{1,0:T(8,128)S(1)} %bitcast.51, bf16[256,2048]{1,0:T(8,128)(2,1)S(1)} %bitcast.57), kind=kOutput, calls=%fused_computation.62 | convolution fusion | flops 12884901888 | bytes 19922944 | tf_op jit(solution)/shard_map/dot_general | solution.py:56
  119.7 5.5 %all-to-all-start.6 = ((f32[8,128,512]{2,1,0:T(8,128)}), f32[8,128,512]{2,1,0:T(8,128)}, u32[]{:S(2)}, u32[]{:S(2)}) async-start(f32[8,128,512]{2,1,0:T(8,128)} %all_to_all.114), calls=%async_computation.6 | async-start | bytes 4194304 | tf_op jit(solution)/shard_map/all_to_all | solution.py:59
  125.2 21.0 %fusion.21 = (bf16[4,64,2048]{2,0,1:T(4,128)(2,1)S(1)}, bf16[4,64,2048]{2,0,1:T(4,128)(2,1)}, bf16[4,64,2048]{2,0,1:T(4,128)(2,1)S(1)}) fusion(f32[7,64,2048]{2,0,1:T(8,128)} %get-tuple-element.5, f32[2048]{0:T(1024)S(1)} %bitcast.63, f32[2048]{0:T(1024)S(1)} %bitcast.65, f32[2048]{0:T(1024)S(1)} %bitcast.67, f32[2048]{0:T(1024)S(1)} %bitcast.61, ...), kind=kLoop, calls=%fused_computation.49 | loop fusion | flops 12582912 | bytes 28344320 | tf_op jit(solution)/shard_map/convert_element_type | solution.py:54
  146.8 10.9 %fusion.28 = f32[2048,256]{1,0:T(8,128)S(1)} fusion(f32[2048,2048]{1,0:T(8,128)} %reshape.131, bf16[256,2048]{1,0:T(8,128)(2,1)S(1)} %bitcast.58), kind=kOutput, calls=%fused_computation.61 | convolution fusion | flops 12884901888 | bytes 19922944 | tf_op jit(solution)/shard_map/dot_general | solution.py:56
  165.2 10.9 %fusion.27 = f32[2048,256]{1,0:T(8,128)S(1)} fusion(f32[2048,2048]{1,0:T(8,128)} %reshape.131, bf16[256,2048]{1,0:T(8,128)(2,1)S(1)} %bitcast.59), kind=kOutput, calls=%fused_computation.60 | convolution fusion | flops 12884901888 | bytes 19922944 | tf_op jit(solution)/shard_map/dot_general | solution.py:56
  177.8 18.0 %all-to-all-done.4 = f32[8,128,512]{2,1,0:T(8,128)} async-done(((f32[8,128,512]{2,1,0:T(8,128)}), f32[8,128,512]{2,1,0:T(8,128)}, u32[]{:S(2)}, u32[]{:S(2)}) %all-to-all-start.4) | async-done | bytes 2097184 | tf_op jit(solution)/shard_map/all_to_all | solution.py:59
  200.9 10.9 %fusion.26 = f32[2048,256]{1,0:T(8,128)S(1)} fusion(f32[2048,2048]{1,0:T(8,128)} %reshape.131, bf16[256,2048]{1,0:T(8,128)(2,1)S(1)} %bitcast.56), kind=kOutput, calls=%fused_computation.59 | convolution fusion | flops 12884901888 | bytes 19922944 | tf_op jit(solution)/shard_map/dot_general | solution.py:56
  213.5 18.1 %all-to-all-done.2 = f32[8,128,512]{2,1,0:T(8,128)} async-done(((f32[8,128,512]{2,1,0:T(8,128)}), f32[8,128,512]{2,1,0:T(8,128)}, u32[]{:S(2)}, u32[]{:S(2)}) %all-to-all-start.2) | async-done | bytes 2097184 | tf_op jit(solution)/shard_map/all_to_all | solution.py:59
  242.0 23.3 %all-to-all-done = f32[8,128,512]{2,1,0:T(8,128)S(1)} async-done(((f32[8,128,512]{2,1,0:T(8,128)}), f32[8,128,512]{2,1,0:T(8,128)S(1)}, u32[]{:S(2)}, u32[]{:S(2)}) %all-to-all-start) | async-done | bytes 2097184 | tf_op jit(solution)/shard_map/all_to_all | solution.py:59
  265.3 9.3 %all-to-all-start.7 = ((f32[16,8,4096]{2,1,0:T(8,128)}), f32[16,8,4096]{2,1,0:T(8,128)}, u32[]{:S(2)}, u32[]{:S(2)}) async-start(f32[16,8,4096]{2,1,0:T(8,128)} %all_to_all.117), calls=%async_computation.7 | async-start | bytes 4194304 | tf_op jit(solution)/shard_map/all_to_all | solution.py:58
  281.5 21.7 %all-to-all-done.7 = f32[16,8,4096]{2,1,0:T(8,128)} async-done(((f32[16,8,4096]{2,1,0:T(8,128)}), f32[16,8,4096]{2,1,0:T(8,128)}, u32[]{:S(2)}, u32[]{:S(2)}) %all-to-all-start.7) | async-done | bytes 2097184 | tf_op jit(solution)/shard_map/all_to_all | solution.py:58
  303.1 7.1 %all-to-all-start.5 = ((f32[16,8,4096]{2,1,0:T(8,128)}), f32[16,8,4096]{2,1,0:T(8,128)}, u32[]{:S(2)}, u32[]{:S(2)}) async-start(f32[16,8,4096]{2,1,0:T(8,128)} %all_to_all.111), calls=%async_computation.5 | async-start | bytes 4194304 | tf_op jit(solution)/shard_map/all_to_all | solution.py:58
  317.2 21.7 %all-to-all-done.5 = f32[16,8,4096]{2,1,0:T(8,128)} async-done(((f32[16,8,4096]{2,1,0:T(8,128)}), f32[16,8,4096]{2,1,0:T(8,128)}, u32[]{:S(2)}, u32[]{:S(2)}) %all-to-all-start.5) | async-done | bytes 2097184 | tf_op jit(solution)/shard_map/all_to_all | solution.py:58
  338.9 7.1 %all-to-all-start.3 = ((f32[16,8,4096]{2,1,0:T(8,128)}), f32[16,8,4096]{2,1,0:T(8,128)}, u32[]{:S(2)}, u32[]{:S(2)}) async-start(f32[16,8,4096]{2,1,0:T(8,128)} %all_to_all.105), calls=%async_computation.3 | async-start | bytes 4194304 | tf_op jit(solution)/shard_map/all_to_all | solution.py:58
  351.3 23.3 %all-to-all-done.3 = f32[16,8,4096]{2,1,0:T(8,128)} async-done(((f32[16,8,4096]{2,1,0:T(8,128)}), f32[16,8,4096]{2,1,0:T(8,128)}, u32[]{:S(2)}, u32[]{:S(2)}) %all-to-all-start.3) | async-done | bytes 2097184 | tf_op jit(solution)/shard_map/all_to_all | solution.py:58
  374.6 7.7 %all-to-all-start.1 = ((f32[16,8,4096]{2,1,0:T(8,128)}), f32[16,8,4096]{2,1,0:T(8,128)}, u32[]{:S(2)}, u32[]{:S(2)}) async-start(f32[16,8,4096]{2,1,0:T(8,128)} %all_to_all.99), calls=%async_computation.1 | async-start | bytes 4194304 | tf_op jit(solution)/shard_map/all_to_all | solution.py:58
  393.4 17.3 %all-to-all-done.1 = f32[16,8,4096]{2,1,0:T(8,128)} async-done(((f32[16,8,4096]{2,1,0:T(8,128)}), f32[16,8,4096]{2,1,0:T(8,128)}, u32[]{:S(2)}, u32[]{:S(2)}) %all-to-all-start.1) | async-done | bytes 2097184 | tf_op jit(solution)/shard_map/all_to_all | solution.py:58
  420.3 5.5 %stack_reshape.13 = f32[8,1,16,8,2,4,64]{6,5,4,3,2,0,1:T(4,128)} reshape(f32[8,16,4096]{2,1,0:T(8,128)} %copy.78) | data formatting | bytes 4194304 | tf_op jit(solution)/shard_map/stack;reshape | solution.py:66
  425.8 5.4 %stack_reshape.14 = f32[8,1,16,8,2,4,64]{6,5,4,3,2,0,1:T(4,128)} reshape(f32[8,16,4096]{2,1,0:T(8,128)} %copy.81) | data formatting | bytes 4194304 | tf_op jit(solution)/shard_map/stack;reshape | solution.py:66
  435.4 9.5 %maximum_bitcast_fusion = f32[8,2,4,16,4,8,64]{6,4,1,5,3,0,2:T(4,128)S(1)} fusion(f32[8,1,16,8,2,4,64]{6,5,4,3,2,0,1:T(4,128)} %stack_reshape.15, f32[8,1,16,8,2,4,64]{6,5,4,3,2,0,1:T(4,128)} %stack_reshape.14, f32[8,1,16,8,2,4,64]{6,5,4,3,2,0,1:T(4,128)} %stack_reshape.13, f32[8,1,16,8,2,4,64]{6,5,4,3,2,0,1:T(4,128)} %stack_reshape.12), kind=kLoop, calls=%fused_computation.1 | loop fusion | flops 6291456 | bytes 16777216 | tf_op jit(solution)/shard_map/transpose | solution.py:67
  444.9 7.0 %copy.85 = f32[8,2,4,16,4,8,64]{6,5,4,3,2,1,0:T(8,128)} copy(f32[8,2,4,16,4,8,64]{6,4,1,5,3,0,2:T(4,128)S(1)} %maximum_bitcast_fusion) | data formatting | bytes 16777216 | tf_op jit(solution)/shard_map/transpose | solution.py:67
  451.9 14.2 %reshape.136 = f32[8,2,256,512]{3,2,1,0:T(8,128)} reshape(f32[8,2,4,16,4,8,64]{6,5,4,3,2,1,0:T(8,128)} %copy.85) | data formatting | bytes 16777216 | tf_op jit(solution)/shard_map/reshape | solution.py:68
  466.2 12.5 %fusion.7 = f32[8,512,512]{2,1,0:T(8,128)} fusion(f32[8,2,256,512]{3,2,1,0:T(8,128)} %reshape.136), kind=kOutput, calls=%fused_computation.17 | convolution fusion | flops 6442450944 | bytes 16777216 | tf_op jit(solution)/shard_map/cma,cmb->cab/dot_general | solution.py:70
  478.7 16.5 %convolution_bitcast_fusion = f32[1,8,512,512]{3,2,1,0:T(8,128)} fusion(f32[8,2,256,512]{3,2,1,0:T(8,128)S(1)} %copy-done), kind=kOutput, calls=%fused_computation.19 | convolution fusion | flops 12884901888 | bytes 16777216 | tf_op jit(solution)/shard_map/cpma,cpmb->cab/dot_general | solution.py:69
  495.3 9.1 %copy.88 = f32[8,512,512]{1,2,0:T(8,128)} copy(f32[8,512,512]{2,1,0:T(8,128)} %fusion.7) | data formatting | bytes 16777216 | tf_op jit(solution)/shard_map/cma,cmb->cab/dot_general | solution.py:70
  504.4 11.1 %fusion.3 = f32[1,8,512,512]{3,2,1,0:T(8,128)} fusion(f32[8,512,512]{2,1,0:T(8,128)} %fusion.7, f32[8,512,512]{1,2,0:T(8,128)} %copy.88), kind=kLoop, calls=%fused_computation.10 | loop fusion | flops 2097152 | bytes 25165824 | tf_op jit(solution)/shard_map/stack | solution.py:72
  515.5 11.9 %maximum_multiply_fusion = f32[2,8,512,512]{3,2,1,0:T(8,128)} fusion(f32[1,8,512,512]{3,2,1,0:T(8,128)} %fusion.3, f32[1,8,512,512]{3,2,1,0:T(8,128)} %convolution_bitcast_fusion), kind=kLoop, calls=%fused_computation.2 | loop fusion | flops 8388608 | bytes 33554432 | tf_op jit(solution)/shard_map/div | solution.py:72
  (53 shorter events, 89.9 us)
Async XLA Ops:
  6.2 41.1 %copy-start.1 = (bf16[8,8,16,2048]{3,2,1,0:T(8,128)(2,1)}, bf16[8,8,16,2048]{3,2,1,0:T(8,128)(2,1)S(1)}, u32[]{:S(2)}) copy-start(bf16[8,8,16,2048]{3,2,1,0:T(8,128)(2,1)S(1)} %copy.92) | copy-start | bytes 12582916
  7.4 88.3 %collective-permute-start = (bf16[3,64,2048]{2,1,0:T(8,128)(2,1)S(1)}, bf16[3,64,2048]{2,1,0:T(8,128)(2,1)S(1)}, u32[]{:S(2)}, u32[]{:S(2)}) collective-permute-start(bf16[3,64,2048]{2,1,0:T(8,128)(2,1)S(1)} %copy.71), channel_id=1, source_target_pairs={{0,1},{1,2},{2,3},{3,4},{4,5},{5,6},{6,7},{7,8},{8,9},{9,10},{10,1... | collective-permute-start | bytes 2359304 | tf_op jit(solution)/shard_map/ppermute | solution.py:15
  75.2 20.5 %copy-start.3 = (s32[4,2048]{1,0:T(4,128)S(1)}, s32[4,2048]{1,0:T(4,128)}, u32[]{:S(2)}) copy-start(s32[4,2048]{1,0:T(4,128)} %param.3) | copy-start | bytes 98308
  96.4 12.0 %slice-start = ((s8[16777216]{0:T(1024)(128)(4,1)}), s8[4194304]{0:T(1024)(128)(4,1)S(1)}, s32[]{:S(2)}) async-start(s8[16777216]{0:T(1024)(128)(4,1)} %bitcast.50), calls=%async_computation.8 | async-start | bytes 8388608
  96.4 12.0 %slice-start.1 = ((s8[16777216]{0:T(1024)(128)(4,1)}), s8[4194304]{0:T(1024)(128)(4,1)S(1)}, s32[]{:S(2)}) async-start(s8[16777216]{0:T(1024)(128)(4,1)} %bitcast.50), calls=%async_computation.9 | async-start | bytes 8388608
  96.4 12.0 %slice-start.2 = ((s8[16777216]{0:T(1024)(128)(4,1)}), s8[4194304]{0:T(1024)(128)(4,1)S(1)}, s32[]{:S(2)}) async-start(s8[16777216]{0:T(1024)(128)(4,1)} %bitcast.50), calls=%async_computation.10 | async-start | bytes 8388608
  105.6 4.1 slice-start.3
  119.7 39.6 %all-to-all-start.6 = ((f32[8,128,512]{2,1,0:T(8,128)}), f32[8,128,512]{2,1,0:T(8,128)}, u32[]{:S(2)}, u32[]{:S(2)}) async-start(f32[8,128,512]{2,1,0:T(8,128)} %all_to_all.114), calls=%async_computation.6 | async-start | bytes 4194304 | tf_op jit(solution)/shard_map/all_to_all | solution.py:59
  159.3 5.3 %copy-start.2 = (bf16[4,64,2048]{2,0,1:T(4,128)(2,1)S(1)}, bf16[4,64,2048]{2,0,1:T(4,128)(2,1)}, u32[]{:S(2)}) copy-start(bf16[4,64,2048]{2,0,1:T(4,128)(2,1)} %get-tuple-element.10) | copy-start | bytes 3145732
  159.3 36.4 %all-to-all-start.4 = ((f32[8,128,512]{2,1,0:T(8,128)}), f32[8,128,512]{2,1,0:T(8,128)}, u32[]{:S(2)}, u32[]{:S(2)}) async-start(f32[8,128,512]{2,1,0:T(8,128)} %all_to_all.108), calls=%async_computation.4 | async-start | bytes 4194304 | tf_op jit(solution)/shard_map/all_to_all | solution.py:59
  195.8 35.8 %all-to-all-start.2 = ((f32[8,128,512]{2,1,0:T(8,128)}), f32[8,128,512]{2,1,0:T(8,128)}, u32[]{:S(2)}, u32[]{:S(2)}) async-start(f32[8,128,512]{2,1,0:T(8,128)} %all_to_all.102), calls=%async_computation.2 | async-start | bytes 4194304 | tf_op jit(solution)/shard_map/all_to_all | solution.py:59
  231.5 33.7 %all-to-all-start = ((f32[8,128,512]{2,1,0:T(8,128)}), f32[8,128,512]{2,1,0:T(8,128)S(1)}, u32[]{:S(2)}, u32[]{:S(2)}) async-start(f32[8,128,512]{2,1,0:T(8,128)} %all_to_all.96), calls=%async_computation | async-start | bytes 4194304 | tf_op jit(solution)/shard_map/all_to_all | solution.py:59
  265.3 37.8 %all-to-all-start.7 = ((f32[16,8,4096]{2,1,0:T(8,128)}), f32[16,8,4096]{2,1,0:T(8,128)}, u32[]{:S(2)}, u32[]{:S(2)}) async-start(f32[16,8,4096]{2,1,0:T(8,128)} %all_to_all.117), calls=%async_computation.7 | async-start | bytes 4194304 | tf_op jit(solution)/shard_map/all_to_all | solution.py:58
  303.1 35.7 %all-to-all-start.5 = ((f32[16,8,4096]{2,1,0:T(8,128)}), f32[16,8,4096]{2,1,0:T(8,128)}, u32[]{:S(2)}, u32[]{:S(2)}) async-start(f32[16,8,4096]{2,1,0:T(8,128)} %all_to_all.111), calls=%async_computation.5 | async-start | bytes 4194304 | tf_op jit(solution)/shard_map/all_to_all | solution.py:58
  338.9 35.7 %all-to-all-start.3 = ((f32[16,8,4096]{2,1,0:T(8,128)}), f32[16,8,4096]{2,1,0:T(8,128)}, u32[]{:S(2)}, u32[]{:S(2)}) async-start(f32[16,8,4096]{2,1,0:T(8,128)} %all_to_all.105), calls=%async_computation.3 | async-start | bytes 4194304 | tf_op jit(solution)/shard_map/all_to_all | solution.py:58
  374.6 36.1 %all-to-all-start.1 = ((f32[16,8,4096]{2,1,0:T(8,128)}), f32[16,8,4096]{2,1,0:T(8,128)}, u32[]{:S(2)}, u32[]{:S(2)}) async-start(f32[16,8,4096]{2,1,0:T(8,128)} %all_to_all.99), calls=%async_computation.1 | async-start | bytes 4194304 | tf_op jit(solution)/shard_map/all_to_all | solution.py:58
  466.2 12.6 %copy-start = (f32[8,2,256,512]{3,2,1,0:T(8,128)S(1)}, f32[8,2,256,512]{3,2,1,0:T(8,128)}, u32[]{:S(2)}) copy-start(f32[8,2,256,512]{3,2,1,0:T(8,128)} %reshape.136) | copy-start | bytes 25165828
where the time goes:
time: 538 us; the launch traced here: 528 us
  local copies, waits for them, and re-layouts  149 us (28%)
  waiting for transfers between devices  143 us (27%)
  other arithmetic  110 us (20%)
  matrix products  70 us (13%)
  starting transfers between devices  55.1 us (10%)
    all_to_all x4, waiting for transfers between devices, on_device(): lax.all_to_all(lax.all_to_all(spectra, 'inp', split_axis=0, concat_axis=1...  83.9 us
    all_to_all x4, waiting for transfers between devices, on_device(): lax.all_to_all(spectra, 'inp', split_axis=0, concat_axis=1, tiled=True)  59.3 us
    dot_general x4, matrix products, on_device(): lax.dot_general(table, filtered, (((1,), (1,)), ((), ())), precision=high...  40.9 us
    mul x1, other arithmetic, dft_table(): -jnp.sin(angle) * scale  34.9 us
    all_to_all x4, starting transfers between devices, on_device(): lax.all_to_all(lax.all_to_all(spectra, 'inp', split_axis=0, concat_axis=1...  31.3 us
    all_to_all x8, local copies, waits for them, and re-layouts, on_device(): lax.all_to_all(lax.all_to_all(spectra, 'inp', split_axis=0, concat_axis=1...  26.4 us
    convert_element_type x2, other arithmetic, on_device(): filtered.astype(jnp.bfloat16)  23.2 us
    all_to_all x8, local copies, waits for them, and re-layouts, on_device(): lax.all_to_all(spectra, 'inp', split_axis=0, concat_axis=1, tiled=True)  21.6 us
  transfers between devices with their start and end apart: 9, of which 7 were waited for; matrix products, arithmetic and copies ran while one was open for 31% of the time, Pallas kernels for 0%

commit v1 on v0

v1 whole, which is shorter than its diff:
```python
import functools

import jax
import jax.numpy as jnp
import ml_dtypes
import numpy as np
from jax import lax
from jax.experimental import pallas as pl
from jax.experimental.pallas import tpu as pltpu
from jax.sharding import PartitionSpec as P

MESH = pl.DeviceIdType.MESH
LANES = 128
GROUP = 16
STRIDE = 53
VMEM = 60 * 2**20


def dft_table(frame_len, devices):
    channels = frame_len // 2
    points = np.arange(frame_len)
    turn = np.arange(channels)[:, None] * points[None, :] % frame_len
    wave = np.cos(2 * np.pi * points / frame_len)
    sine = np.sin(2 * np.pi * points / frame_len)
    rows = np.stack([wave[turn], -sine[turn]], axis=1)
    rows = rows.reshape(devices, 2 * channels // devices, frame_len)
    high = rows.astype(ml_dtypes.bfloat16)
    low = (rows - high.astype(np.float64)).astype(ml_dtypes.bfloat16)
    return np.stack([high, low])


def peer(step, total):
    inp, tm = lax.axis_index("inp"), lax.axis_index("tm")
    offset = (step * STRIDE) % total
    x = (inp // 2 + offset // 32) % 4
    y = ((tm // 8) * 2 + inp % 2 + (offset // 8) % 4) % 4
    z = ((tm // 2) % 4 + (offset // 2) % 4) % 4
    core = (tm + offset) % 2
    return x * 2 + y % 2, (y // 2) * 8 + z * 2 + core


def spectra_kernel(
    total,
    samples,
    taps,
    table,
    arrived,
    raw,
    past_out,
    past_in,
    filtered,
    tab,
    stage,
    outbox,
    raw_sem,
    tab_sem,
    past_sem,
    send_sem,
    recv_sem,
    own_sem,
):
    inputs = samples.shape[0]
    tap_count, frame_len = taps.shape
    spec_dev = samples.shape[1] // frame_len
    tm_count = lax.axis_size("tm")
    back = tap_count - 1
    half = spec_dev // 2
    rows = half * inputs
    inp, tm = lax.axis_index("inp"), lax.axis_index("tm")
    me = inp * tm_count + tm
    tiles = half * inputs // LANES
    msg = outbox.shape[2]

    def load(part, first, count):
        cut = pl.ds(first * frame_len, count * frame_len)
        return pltpu.make_async_copy(samples.at[:, cut], raw.at[:, cut], raw_sem.at[part])

    parts = [(spec_dev - back, back), (half - back, spec_dev - half), (0, half - back)]
    for part, (first, count) in enumerate(parts[:2]):
        load(part, first, count).start()

    def fetch(group):
        def one(k, carry):
            step = group * GROUP + k
            to_inp, to_tm = peer(step, total)
            pltpu.make_async_copy(
                table.at[:, to_inp * tm_count + to_tm], tab.at[:, step], tab_sem.at[group]
            ).start()
            return carry

        lax.fori_loop(0, GROUP, one, 0)

    fetch(0)
    load(2, *parts[2]).start()

    barrier = pltpu.get_barrier_semaphore()

    def greet(step, carry):
        pl.semaphore_signal(barrier, inc=1, device_id=peer(step, total), device_id_type=MESH)
        return carry

    lax.fori_loop(1, total, greet, 0)

    weights_of = lambda cut: [
        taps[k : k + 1, cut].astype(jnp.float32) for k in range(tap_count)
    ]

    def fir(first, count):
        def tile(n, carry):
            cut = pl.ds(pl.multiple_of(n * LANES, LANES), LANES)
            weights = weights_of(cut)

            def frame(s):
                if s < 0:
                    return past_in[(s + back) * inputs : (s + back + 1) * inputs, cut].astype(
                        jnp.float32
                    )
                at = pl.ds(pl.multiple_of(s * frame_len + n * LANES, LANES), LANES)
                return raw[:, at].astype(jnp.float32)

            window = [frame(first - back + k) for k in range(back)]
            for s in range(first, first + count):
                window.append(frame(s))
                value = weights[0] * window[0]
                for k in range(1, tap_count):
                    value = value + weights[k] * window[k]
                filtered[s * inputs : (s + 1) * inputs, cut] = value.astype(jnp.bfloat16)
                window.pop(0)
            return carry

        lax.fori_loop(0, frame_len // LANES, tile, 0)

    load(0, *parts[0]).wait()
    for k in range(back):
        first = (spec_dev - back + k) * frame_len
        past_out[k * inputs : (k + 1) * inputs, :] = (
            raw[:, first : first + frame_len].astype(jnp.float32).astype(jnp.bfloat16)
        )
    load(1, *parts[1]).wait()
    fir(half, half)

    pl.semaphore_wait(barrier, total - 1)
    past = pltpu.make_async_remote_copy(
        past_out,
        past_in,
        past_sem.at[0],
        past_sem.at[1],
        device_id=(inp, lax.rem(tm + 1, tm_count)),
        device_id_type=MESH,
    )

    @pl.when(tm < tm_count - 1)
    def _():
        past.start()

    for group in range(1, total // GROUP):
        fetch(group)

    def own(phase):
        return pltpu.make_async_copy(
            outbox.at[phase, 0], arrived.at[phase, me], own_sem.at[phase]
        )

    def channelize(phase, base):
        def group_step(group, carry):
            at = pl.ds(group * GROUP, GROUP)
            if phase == 0:
                pltpu.make_async_copy(tab.at[:, at], tab.at[:, at], tab_sem.at[group]).wait()
            frames = filtered[base : base + rows, :]
            value = None
            for part in range(2):
                lhs = tab[part, at].reshape(-1, frame_len)
                term = lax.dot_general(
                    lhs, frames, (((1,), (1,)), ((), ())), preferred_element_type=jnp.float32
                )
                value = term if value is None else value + term
            height = value.shape[0]
            for j in range(tiles):
                stage[pl.ds(j, height, stride=tiles), :] = value[:, j * LANES : (j + 1) * LANES]
            outbox[phase, at] = stage[...].reshape(GROUP, msg, LANES).astype(jnp.bfloat16)

            def send(k, carry):
                step = group * GROUP + k

                @pl.when(step == 0)
                def _():
                    own(phase).start()

                @pl.when(step > 0)
                def _():
                    pltpu.make_async_remote_copy(
                        outbox.at[phase, step],
                        arrived.at[phase, me],
                        send_sem.at[phase],
                        recv_sem.at[phase],
                        device_id=peer(step, total),
                        device_id_type=MESH,
                    ).start()

                return carry

            lax.fori_loop(0, GROUP, send, 0)
            return carry

        lax.fori_loop(0, total // GROUP, group_step, 0)

    channelize(0, rows)

    @pl.when(tm > 0)
    def _():
        pltpu.make_async_copy(past_in, past_in, past_sem.at[1]).wait()

    @pl.when(tm == 0)
    def _():
        past_in[...] = jnp.zeros_like(past_in)

    load(2, *parts[2]).wait()
    fir(0, half)
    channelize(1, 0)

    others = pl.ds(0, total - 1)
    for phase in range(2):
        own(phase).wait()
        sent, came = outbox.at[phase, others], arrived.at[phase, others]
        pltpu.make_async_copy(sent, sent, send_sem.at[phase]).wait()
        pltpu.make_async_copy(came, came, recv_sem.at[phase]).wait()

    @pl.when(tm < tm_count - 1)
    def _():
        pltpu.make_async_copy(past_out, past_out, past_sem.at[0]).wait()


def correlate_kernel(inputs, scale, arrived, out):
    phases, sources, rows, _ = arrived.shape
    pair = rows // 8
    lane_sets = LANES // inputs
    inp_count = out.shape[-1] // inputs
    times = sources // inp_count
    lane = lax.broadcasted_iota(jnp.int32, (1, 1, 1, LANES), 3)
    row = lax.broadcasted_iota(jnp.int32, (1, 1, 8, 1), 2)
    sign = jnp.where(row < 4, -1.0, 1.0).astype(jnp.float32)
    del lane_sets

    for c in range(pair):
        columns, turned = [], []
        for i in range(0, inp_count, 2):
            block = arrived[:, i * times : (i + 2) * times, :, :].astype(jnp.float32)
            block = block[:, :, c * 8 : (c + 1) * 8, :]
            even, odd = block[:, :times], block[:, times:]
            shape = even.shape
            flip = lambda v: pltpu.roll(v.reshape(-1, LANES), inputs, 1).reshape(shape)
            low = jnp.where(lane < inputs, even, flip(odd))
            high = jnp.where(lane < inputs, flip(even), odd)
            merged = jnp.concatenate([low, high], axis=0).reshape(-1, times, 8, LANES)
            swapped = jnp.concatenate([merged[:, :, 4:], merged[:, :, :4]], axis=2) * sign
            columns.append(merged.reshape(-1, LANES).astype(jnp.bfloat16))
            turned.append(swapped.reshape(-1, LANES).astype(jnp.bfloat16))
        spectra = jnp.concatenate(columns, axis=1)
        quarter = jnp.concatenate(turned, axis=1)
        across = spectra.T
        out[0, c] = jnp.dot(across, spectra, preferred_element_type=jnp.float32) * scale
        out[1, c] = jnp.dot(across, quarter, preferred_element_type=jnp.float32) * scale


def on_device(table, samples, filter_taps):
    inputs = samples.shape[0]
    tap_count, frame_len = filter_taps.shape
    spec_dev = samples.shape[1] // frame_len
    inp_count, tm_count = lax.axis_size("inp"), lax.axis_size("tm")
    total = inp_count * tm_count
    chan_dev = frame_len // 2 // total
    groups = total // GROUP
    tiles = spec_dev // 2 * inputs // LANES
    msg = 2 * chan_dev * tiles
    bf16 = jnp.bfloat16
    arrived = pl.pallas_call(
        functools.partial(spectra_kernel, total),
        out_shape=jax.ShapeDtypeStruct((2, total, msg, LANES), bf16),
        in_specs=[
            pl.BlockSpec(memory_space=pl.ANY),
            pl.BlockSpec(memory_space=pltpu.VMEM),
            pl.BlockSpec(memory_space=pl.ANY),
        ],
        out_specs=pl.BlockSpec(memory_space=pl.ANY),
        scratch_shapes=[
            pltpu.VMEM(samples.shape, jnp.int32),
            pltpu.VMEM(((tap_count - 1) * inputs, frame_len), bf16),
            pltpu.VMEM(((tap_count - 1) * inputs, frame_len), bf16),
            pltpu.VMEM((spec_dev * inputs, frame_len), bf16),
            pltpu.VMEM((2, total, 2 * chan_dev, frame_len), bf16),
            pltpu.VMEM((GROUP * msg, LANES), jnp.float32),
            pltpu.VMEM((2, total, msg, LANES), bf16),
            pltpu.SemaphoreType.DMA((3,)),
            pltpu.SemaphoreType.DMA((groups,)),
            pltpu.SemaphoreType.DMA((2,)),
            pltpu.SemaphoreType.DMA((2,)),
            pltpu.SemaphoreType.DMA((2,)),
            pltpu.SemaphoreType.DMA((2,)),
        ],
        compiler_params=pltpu.CompilerParams(
            collective_id=0, has_side_effects=True, vmem_limit_bytes=VMEM
        ),
        name="channelize_and_exchange",
    )(samples, filter_taps, table)

    scale = 1.0 / (16384.0**2 * frame_len * spec_dev * tm_count)
    all_inputs = inputs * inp_count
    pairs = chan_dev // 2
    return pl.pallas_call(
        functools.partial(correlate_kernel, inputs, scale),
        grid=(pairs,),
        out_shape=jax.ShapeDtypeStruct((2, chan_dev, all_inputs, all_inputs), jnp.float32),
        in_specs=[pl.BlockSpec((2, total, msg // pairs, LANES), lambda g: (0, 0, g, 0))],
        out_specs=pl.BlockSpec((2, 2, all_inputs, all_inputs), lambda g: (0, g, 0, 0)),
        compiler_params=pltpu.CompilerParams(vmem_limit_bytes=VMEM),
        name="correlate",
    )(arrived)


def solution(mesh):
    devices = mesh.size
    table = dft_table(2048, devices)

    def whole(samples, filter_taps):
        return jax.shard_map(
            on_device,
            mesh=mesh,
            in_specs=(P(), P("inp", "tm"), P()),
            out_specs=P(None, ("inp", "tm"), None, None),
            check_vma=False,
        )(jnp.asarray(table), samples, filter_taps)

    return whole
```

time: 538 us -> 103 us (0.19); the launches traced: 528 us -> 101 us
  local copies, waits for them, and re-layouts: 149 us -> 0 us
  waiting for transfers between devices: 143 us -> 0 us
  other arithmetic: 110 us -> 0 us
  Pallas kernels: 0 us -> 101 us
  matrix products: 70 us -> 0 us
  starting transfers between devices: 55.1 us -> 0 us
    all_to_all x8 -> x0, waiting for transfers between devices: 143 us -> none  [the longest x4 83.9 us: on_device(): lax.all_to_all(lax.all_to_all(spectra, 'inp', split_axis=0, concat_axis=1...]
    pallas_call x0 -> x2, Pallas kernels: none -> 101 us  [the longest x1 91 us: on_device(): pl.pallas_call(functools.partial(spectra_kernel, total), out_shape=jax.Sh...]
    dot_general x6 -> x0, matrix products: 70 us -> none  [the longest x4 40.9 us: on_device(): lax.dot_general(table, filtered, (((1,), (1,)), ((), ())), precision=high...]
    all_to_all x8 -> x0, starting transfers between devices: 50.1 us -> none  [the longest x4 31.3 us: on_device(): lax.all_to_all(lax.all_to_all(spectra, 'inp', split_axis=0, concat_axis=1...]
    all_to_all x16 -> x0, local copies, waits for them, and re-layouts: 48 us -> none  [the longest x8 26.4 us: on_device(): lax.all_to_all(lax.all_to_all(spectra, 'inp', split_axis=0, concat_axis=1...]
    another operation x5 -> x0, local copies, waits for them, and re-layouts: 41.8 us -> none  [the longest x1 21.3 us: dft_table(): jnp.stack([jnp.cos(angle) * scale, -jnp.sin(angle) * scale], axis=1)]
    convert_element_type x4 -> x0, other arithmetic: 36.1 us -> none  [the longest x2 23.2 us: on_device(): filtered.astype(jnp.bfloat16)]
    mul x1 -> x0, other arithmetic: 34.9 us -> none  [dft_table(): -jnp.sin(angle) * scale]
  transfers between devices with their start and end apart: 9 -> 0, of which waited for: 7 -> 0; matrix products, arithmetic and copies ran while one was open for 31% -> 0% of each run, Pallas kernels for 0% -> 0%
where the time goes in v1:
time: 103 us; the launch traced here: 101 us
  Pallas kernels  101 us (98%)
    pallas_call x1, Pallas kernels, on_device(): pl.pallas_call(functools.partial(spectra_kernel, total), out_shape=jax.Sh...  91 us
    pallas_call x1, Pallas kernels, on_device(): pl.pallas_call(functools.partial(correlate_kernel, inputs, scale), grid=(...  10.4 us

profile of v1, /device:TPU:1, one launch (start us, length us, event | category | flops | bytes accessed | tf_op | source)
XLA Modules:
  0.0 101.4 jit_solution(1003242962470466052)
XLA Ops:
  0.0 91.0 %channelize_and_exchange.1.arrived = bf16[2,128,64,128]{3,2,1,0:T(8,128)(2,1)} custom-call(s32[64,32768]{1,0:T(8,128)} %samples.1, s32[4,2048]{1,0:T(4,128)} %taps.1, bf16[2,128,16,2048]{3,2,1,0:T(8,128)(2,1)} %constant.2.clone.table), custom_call_target="tpu_custom_call" | custom-call | tf_op jit(solution)/shard_map/channelize_and_exchange/pallas_call | solution.py:276
  91.0 10.4 %correlate.1 = f32[2,8,512,512]{3,2,1,0:T(8,128)} custom-call(bf16[2,128,64,128]{3,2,1,0:T(8,128)(2,1)} %channelize_and_exchange.1.arrived), custom_call_target="tpu_custom_call" | custom-call | tf_op jit(solution)/shard_map/correlate/pallas_call | solution.py:309

commit v2 on v1

--- a/solution.py
+++ b/solution.py
@@ -12,7 +12,8 @@
 MESH = pl.DeviceIdType.MESH
 LANES = 128
 GROUP = 16
-STRIDE = 53
+STRIDE = 11
+PIECE = 32
 VMEM = 60 * 2**20
 
 
@@ -31,12 +32,16 @@
 
 def peer(step, total):
     inp, tm = lax.axis_index("inp"), lax.axis_index("tm")
-    offset = (step * STRIDE) % total
-    x = (inp // 2 + offset // 32) % 4
-    y = ((tm // 8) * 2 + inp % 2 + (offset // 8) % 4) % 4
-    z = ((tm // 2) % 4 + (offset // 2) % 4) % 4
-    core = (tm + offset) % 2
-    return x * 2 + y % 2, (y // 2) * 8 + z * 2 + core
+    plane = total // 4
+    rest = lax.max(step - plane, 0)
+    far = step >= plane
+    dz = jnp.where(far, 1 + lax.rem(rest, 3), 0)
+    mixed = lax.rem(jnp.where(far, lax.div(rest, 3), step) * STRIDE, plane)
+    x = lax.rem(lax.div(inp, 2) + lax.div(mixed, 8), 4)
+    y = lax.rem(lax.div(tm, 8) * 2 + lax.rem(inp, 2) + lax.rem(lax.div(mixed, 2), 4), 4)
+    z = lax.rem(lax.div(tm, 2) + dz, 4)
+    core = lax.rem(tm + mixed, 2)
+    return x * 2 + lax.rem(y, 2), lax.div(y, 2) * 8 + z * 2 + core
 
 
 def spectra_kernel(
@@ -136,22 +141,26 @@
         past_out[k * inputs : (k + 1) * inputs, :] = (
             raw[:, first : first + frame_len].astype(jnp.float32).astype(jnp.bfloat16)
         )
+    def hand_on(piece):
+        cut = pl.ds(piece * PIECE, PIECE)
+        return pltpu.make_async_remote_copy(
+            past_out.at[cut],
+            past_in.at[cut],
+            past_sem.at[0],
+            past_sem.at[1],
+            device_id=(inp, lax.rem(tm + 1, tm_count)),
+            device_id_type=MESH,
+        )
+
+    pl.semaphore_wait(barrier, total - 1)
+
+    @pl.when(tm < tm_count - 1)
+    def _():
+        for piece in range(back * inputs // PIECE):
+            hand_on(piece).start()
+
     load(1, *parts[1]).wait()
     fir(half, half)
-
-    pl.semaphore_wait(barrier, total - 1)
-    past = pltpu.make_async_remote_copy(
-        past_out,
-        past_in,
-        past_sem.at[0],
-        past_sem.at[1],
-        device_id=(inp, lax.rem(tm + 1, tm_count)),
-        device_id_type=MESH,
-    )
-
-    @pl.when(tm < tm_count - 1)
-    def _():
-        past.start()
 
     for group in range(1, total // GROUP):
         fetch(group)

time: 103 us -> 88.2 us (0.86)
  Pallas kernels: 101 us -> 86.8 us
    pallas_call x1, Pallas kernels: 91 us -> 76.4 us  [on_device(): pl.pallas_call(functools.partial(spectra_kernel, total), out_shape=jax.Sh...]
where the time goes in v2:
time: 88.2 us; the launch traced here: 86.8 us
  Pallas kernels  86.8 us (98%)
    pallas_call x1, Pallas kernels, on_device(): pl.pallas_call(functools.partial(spectra_kernel, total), out_shape=jax.Sh...  76.4 us
    pallas_call x1, Pallas kernels, on_device(): pl.pallas_call(functools.partial(correlate_kernel, inputs, scale), grid=(...  10.4 us

profile of v2, /device:TPU:1, one launch (start us, length us, event | category | flops | bytes accessed | tf_op | source)
XLA Modules:
  0.0 86.8 jit_solution(17930818400860426343)
XLA Ops:
  0.0 76.4 %channelize_and_exchange.1.arrived = bf16[2,128,64,128]{3,2,1,0:T(8,128)(2,1)} custom-call(s32[64,32768]{1,0:T(8,128)} %samples.1, s32[4,2048]{1,0:T(4,128)} %taps.1, bf16[2,128,16,2048]{3,2,1,0:T(8,128)(2,1)} %constant.2.clone.table), custom_call_target="tpu_custom_call" | custom-call | tf_op jit(solution)/shard_map/channelize_and_exchange/pallas_call | solution.py:285
  76.5 10.4 %correlate.1 = f32[2,8,512,512]{3,2,1,0:T(8,128)} custom-call(bf16[2,128,64,128]{3,2,1,0:T(8,128)(2,1)} %channelize_and_exchange.1.arrived), custom_call_target="tpu_custom_call" | custom-call | tf_op jit(solution)/shard_map/correlate/pallas_call | solution.py:318

commit v3 on v2

v3 whole, which is shorter than its diff:
```python
import functools

import jax
import jax.numpy as jnp
import ml_dtypes
import numpy as np
from jax import lax
from jax.experimental import pallas as pl
from jax.experimental.pallas import tpu as pltpu
from jax.sharding import PartitionSpec as P

MESH = pl.DeviceIdType.MESH
LANES = 128
QUAD = 4
GROUP = 16
STRIDE = 11
PIECE = 32
VMEM = 44 * 2**20


def dft_table(frame_len, devices):
    channels = frame_len // 2
    points = np.arange(frame_len)
    turn = np.arange(channels)[:, None] * points[None, :] % frame_len
    wave = np.cos(2 * np.pi * points / frame_len)
    sine = np.sin(2 * np.pi * points / frame_len)
    rows = np.stack([wave[turn], -sine[turn]])
    high = rows.astype(ml_dtypes.bfloat16)
    low = (rows - high.astype(np.float64)).astype(ml_dtypes.bfloat16)
    parts = np.stack([high, low]).reshape(2, 2, devices, 2, QUAD, frame_len)
    return parts.transpose(3, 2, 0, 1, 4, 5).reshape(2, devices, 4 * QUAD, frame_len)


def peer(step, total):
    inp, tm = lax.axis_index("inp"), lax.axis_index("tm")
    plane = total // 4
    rest = lax.max(step - plane, 0)
    far = step >= plane
    dz = jnp.where(far, 1 + lax.rem(rest, 3), 0)
    mixed = lax.rem(jnp.where(far, lax.div(rest, 3), step) * STRIDE, plane)
    x = lax.rem(lax.div(inp, 2) + lax.div(mixed, 8), 4)
    y = lax.rem(lax.div(tm, 8) * 2 + lax.rem(inp, 2) + lax.rem(lax.div(mixed, 2), 4), 4)
    z = lax.rem(lax.div(tm, 2) + dz, 4)
    core = lax.rem(tm + mixed, 2)
    return x * 2 + lax.rem(y, 2), lax.div(y, 2) * 8 + z * 2 + core


def interleave(value):
    sets = [value[:, :, j * LANES : (j + 1) * LANES] for j in range(QUAD)]
    row = lax.broadcasted_iota(jnp.int32, (1, 8, 1), 1)

    def exchange(first, second, reach):
        keep = lax.rem(lax.div(row, reach), 2) == 0
        low = jnp.where(keep, first, pltpu.roll(second, reach, 1))
        high = jnp.where(keep, pltpu.roll(first, 8 - reach, 1), second)
        return low, high

    near, far = zip(exchange(sets[0], sets[2], 2), exchange(sets[1], sets[3], 2))
    near, far = (near[0], far[0]), (near[1], far[1])
    channels = [*exchange(near[0], far[0], 1), *exchange(near[1], far[1], 1)]
    return jnp.concatenate(channels, axis=1)


def correlate(first, second, scale, vis, at):
    all_inputs = vis.shape[-1]
    sources = first.shape[0]
    inputs = LANES // 2
    inp_count = all_inputs // inputs
    times = sources // inp_count
    lane = lax.broadcasted_iota(jnp.int32, (1, 1, LANES), 2)
    row = lax.broadcasted_iota(jnp.int32, (1, 8, 1), 1)
    sign = jnp.where(row < QUAD, -1.0, 1.0).astype(jnp.float32)
    for c in range(2):
        columns, turned = [], []
        for i in range(0, inp_count, 2):
            low, high = [], []
            for ref in (first, second):
                block = ref[i * times : (i + 2) * times].astype(jnp.float32)
                block = block[:, c * 8 : (c + 1) * 8, :]
                even, odd = block[:times], block[times:]
                low.append(jnp.where(lane < inputs, even, pltpu.roll(odd, inputs, 2)))
                high.append(jnp.where(lane < inputs, pltpu.roll(even, inputs, 2), odd))
            merged = jnp.concatenate(low + high, axis=0)
            swapped = pltpu.roll(merged, QUAD, 1) * sign
            columns.append(merged.reshape(-1, LANES).astype(jnp.bfloat16))
            turned.append(swapped.reshape(-1, LANES).astype(jnp.bfloat16))
        spectra = jnp.concatenate(columns, axis=1)
        quarter = jnp.concatenate(turned, axis=1)
        across = spectra.T
        vis[0, at + c] = jnp.dot(across, spectra, preferred_element_type=jnp.float32) * scale
        vis[1, at + c] = jnp.dot(across, quarter, preferred_element_type=jnp.float32) * scale


def correlate_half(half, early, late, scale, vis, done=None):
    def pair(k, carry):
        rows = pl.ds(pl.multiple_of(k * 16, 16), 16)
        early_rows = pl.ds(pl.multiple_of(half * 8 * QUAD + k * 16, 16), 16)
        correlate(early.at[:, early_rows], late.at[half, :, rows], scale, vis, 2 * k)
        if done is not None:
            done(k)
        return carry

    lax.fori_loop(0, QUAD // 2, pair, 0)


def spectra_kernel(
    total,
    scale,
    samples,
    taps,
    table,
    early,
    late,
    vis,
    raw,
    past_out,
    past_in,
    filtered,
    tab,
    early_box,
    late_box,
    raw_sem,
    tab_sem,
    past_sem,
    send_sem,
    recv_sem,
    own_sem,
):
    inputs = samples.shape[0]
    tap_count, frame_len = taps.shape
    spec_dev = samples.shape[1] // frame_len
    tm_count = lax.axis_size("tm")
    back = tap_count - 1
    half = spec_dev // 2
    rows = half * inputs
    inp, tm = lax.axis_index("inp"), lax.axis_index("tm")
    me = inp * tm_count + tm
    groups = total // GROUP

    def load(part, first, count):
        cut = pl.ds(first * frame_len, count * frame_len)
        return pltpu.make_async_copy(samples.at[:, cut], raw.at[:, cut], raw_sem.at[part])

    parts = [(spec_dev - back, back), (half - back, spec_dev - half), (0, half - back)]
    for part, (first, count) in enumerate(parts[:2]):
        load(part, first, count).start()

    def fetch(group):
        def one(k, carry):
            step = group * GROUP + k
            to_inp, to_tm = peer(step, total)
            pltpu.make_async_copy(
                table.at[:, to_inp * tm_count + to_tm], tab.at[:, step], tab_sem.at[group]
            ).start()
            return carry

        lax.fori_loop(0, GROUP, one, 0)

    fetch(0)
    load(2, *parts[2]).start()

    barrier = pltpu.get_barrier_semaphore()

    def greet(step, carry):
        pl.semaphore_signal(barrier, inc=1, device_id=peer(step, total), device_id_type=MESH)
        return carry

    lax.fori_loop(1, total, greet, 0)

    weights_of = lambda cut: [
        taps[k : k + 1, cut].astype(jnp.float32) for k in range(tap_count)
    ]

    def fir(first, count):
        def tile(n, carry):
            cut = pl.ds(pl.multiple_of(n * LANES, LANES), LANES)
            weights = weights_of(cut)

            def frame(s):
                if s < 0:
                    return past_in[(s + back) * inputs : (s + back + 1) * inputs, cut].astype(
                        jnp.float32
                    )
                at = pl.ds(pl.multiple_of(s * frame_len + n * LANES, LANES), LANES)
                return raw[:, at].astype(jnp.float32)

            window = [frame(first - back + k) for k in range(back)]
            for s in range(first, first + count):
                window.append(frame(s))
                value = weights[0] * window[0]
                for k in range(1, tap_count):
                    value = value + weights[k] * window[k]
                filtered[s * inputs : (s + 1) * inputs, cut] = value.astype(jnp.bfloat16)
                window.pop(0)
            return carry

        lax.fori_loop(0, frame_len // LANES, tile, 0)

    load(0, *parts[0]).wait()
    for k in range(back):
        first = (spec_dev - back + k) * frame_len
        past_out[k * inputs : (k + 1) * inputs, :] = (
            raw[:, first : first + frame_len].astype(jnp.float32).astype(jnp.bfloat16)
        )
    def hand_on(piece):
        cut = pl.ds(piece * PIECE, PIECE)
        return pltpu.make_async_remote_copy(
            past_out.at[cut],
            past_in.at[cut],
            past_sem.at[0],
            past_sem.at[1],
            device_id=(inp, lax.rem(tm + 1, tm_count)),
            device_id_type=MESH,
        )

    pl.semaphore_wait(barrier, total - 1)

    @pl.when(tm < tm_count - 1)
    def _():
        for piece in range(back * inputs // PIECE):
            hand_on(piece).start()

    load(1, *parts[1]).wait()
    fir(half, half)

    boxes = [
        (lambda step: early_box.at[step], lambda: early.at[me], early_box, early),
        (lambda step: late_box.at[0, step], lambda: late.at[0, me], late_box.at[0], late.at[0]),
        (lambda step: late_box.at[1, step], lambda: late.at[1, me], late_box.at[1], late.at[1]),
    ]

    def own(phase):
        source, target = boxes[phase][:2]
        return pltpu.make_async_copy(source(0), target(), own_sem.at[phase])

    def channelize(phase, base, halves):
        source, target = boxes[phase][:2]

        def group_step(index, carry):
            group = index if phase == 0 else lax.rem(index * 3 + 2, groups)
            at = pl.ds(group * GROUP, GROUP)
            if phase == 0:

                pltpu.make_async_copy(tab.at[:, at], tab.at[:, at], tab_sem.at[group]).wait()
            frames = filtered[base : base + rows, :]
            for h in halves:
                value = lax.dot_general(
                    tab[h, at].reshape(-1, frame_len),
                    frames,
                    (((1,), (1,)), ((), ())),
                    preferred_element_type=jnp.float32,
                ).reshape(GROUP, 2, 2 * QUAD, -1)
                box = interleave(value[:, 0] + value[:, 1]).astype(jnp.bfloat16)
                if phase == 0:
                    early_box[at, h * 8 * QUAD : (h + 1) * 8 * QUAD] = box
                else:
                    late_box[h, at] = box

            def send(k, carry):
                step = group * GROUP + k

                @pl.when(step == 0)
                def _():
                    own(phase).start()

                @pl.when(step > 0)
                def _():
                    pltpu.make_async_remote_copy(
                        source(step),
                        target(),
                        send_sem.at[phase],
                        recv_sem.at[phase],
                        device_id=peer(step, total),
                        device_id_type=MESH,
                    ).start()

                return carry

            lax.fori_loop(0, GROUP, send, 0)
            return carry

        lax.fori_loop(0, groups, group_step, 0)

    for g in range(1, groups):
        fetch(g)
    channelize(0, rows, (0, 1))

    @pl.when(tm > 0)
    def _():
        pltpu.make_async_copy(past_in, past_in, past_sem.at[1]).wait()

    @pl.when(tm == 0)
    def _():
        past_in[...] = jnp.zeros_like(past_in)

    load(2, *parts[2]).wait()
    fir(0, half)
    channelize(1, 0, (0,))
    channelize(2, 0, (1,))

    others = pl.ds(0, total - 1)

    def arrive(phase):
        came = boxes[phase][3].at[others]
        own(phase).wait()
        pltpu.make_async_copy(came, came, recv_sem.at[phase]).wait()

    arrive(0)
    arrive(1)
    correlate_half(0, early, late, scale, vis)
    arrive(2)
    for phase in range(3):
        sent = boxes[phase][2].at[others]
        pltpu.make_async_copy(sent, sent, send_sem.at[phase]).wait()

    @pl.when(tm < tm_count - 1)
    def _():
        pltpu.make_async_copy(past_out, past_out, past_sem.at[0]).wait()


def correlate_kernel(scale, early, late, vis, out, rest, sem):
    def write(source, k, first):
        pair = pl.ds(2 * k, 2)
        return pltpu.make_async_copy(source.at[:, pair], out.at[:, pl.ds(first + 2 * k, 2)], sem)

    def begin(k, carry):
        write(vis, k, 0).start()
        return carry

    lax.fori_loop(0, QUAD // 2, begin, 0)
    correlate_half(1, early, late, scale, rest, lambda k: write(rest, k, QUAD).start())
    pltpu.make_async_copy(out, out, sem).wait()


def on_device(table, samples, filter_taps):
    inputs = samples.shape[0]
    tap_count, frame_len = filter_taps.shape
    spec_dev = samples.shape[1] // frame_len
    inp_count, tm_count = lax.axis_size("inp"), lax.axis_size("tm")
    total = inp_count * tm_count
    chan_dev = frame_len // 2 // total
    groups = total // GROUP
    all_inputs = inputs * inp_count
    bf16 = jnp.bfloat16
    scale = 1.0 / (16384.0**2 * frame_len * spec_dev * tm_count)
    early_shape = (total, 16 * QUAD, LANES)
    late_shape = (2, total, 8 * QUAD, LANES)
    vis_shape = (2, QUAD, all_inputs, all_inputs)
    hbm = pl.BlockSpec(memory_space=pltpu.HBM)
    vmem = pl.BlockSpec(memory_space=pltpu.VMEM)
    early, late, vis = pl.pallas_call(
        functools.partial(spectra_kernel, total, scale),
        out_shape=[
            pltpu.VMEM(early_shape, bf16),
            pltpu.VMEM(late_shape, bf16),
            pltpu.VMEM(vis_shape, jnp.float32),
        ],
        in_specs=[hbm, vmem, hbm],
        out_specs=[vmem, vmem, vmem],
        scratch_shapes=[
            pltpu.VMEM(samples.shape, jnp.int32),
            pltpu.VMEM(((tap_count - 1) * inputs, frame_len), bf16),
            pltpu.VMEM(((tap_count - 1) * inputs, frame_len), bf16),
            pltpu.VMEM((spec_dev * inputs, frame_len), bf16),
            pltpu.VMEM((2, total, 4 * QUAD, frame_len), bf16),
            pltpu.VMEM(early_shape, bf16),
            pltpu.VMEM(late_shape, bf16),
            pltpu.SemaphoreType.DMA((3,)),
            pltpu.SemaphoreType.DMA((groups,)),
            pltpu.SemaphoreType.DMA((2,)),
            pltpu.SemaphoreType.DMA((3,)),
            pltpu.SemaphoreType.DMA((3,)),
            pltpu.SemaphoreType.DMA((3,)),
        ],
        compiler_params=pltpu.CompilerParams(
            collective_id=0, has_side_effects=True, vmem_limit_bytes=VMEM
        ),
        name="channelize_and_exchange",
    )(samples, filter_taps, table)
    return pl.pallas_call(
        functools.partial(correlate_kernel, scale),
        out_shape=jax.ShapeDtypeStruct((2, chan_dev, all_inputs, all_inputs), jnp.float32),
        in_specs=[vmem, vmem, vmem],
        out_specs=hbm,
        scratch_shapes=[pltpu.VMEM(vis_shape, jnp.float32), pltpu.SemaphoreType.DMA],
        compiler_params=pltpu.CompilerParams(vmem_limit_bytes=VMEM // 2),
        name="correlate",
    )(early, late, vis)


def solution(mesh):
    devices = mesh.size
    table = dft_table(2048, devices)

    def whole(samples, filter_taps):
        return jax.shard_map(
            on_device,
            mesh=mesh,
            in_specs=(P(), P("inp", "tm"), P()),
            out_specs=P(None, ("inp", "tm"), None, None),
            check_vma=False,
        )(jnp.asarray(table), samples, filter_taps)

    return whole
```

time: 88.2 us -> 82.8 us (0.939); the launches traced: 86.8 us -> 82.6 us
  Pallas kernels: 86.8 us -> 82.6 us
    pallas_call x2, Pallas kernels: 86.8 us -> 82.6 us  [the longest x1 76.7 us: on_device(): pl.pallas_call(functools.partial(spectra_kernel, total, scale), out_shape...]
where the time goes in v3:
time: 82.8 us; the launch traced here: 82.6 us
  Pallas kernels  82.6 us (100%)
    pallas_call x1, Pallas kernels, on_device(): pl.pallas_call(functools.partial(spectra_kernel, total, scale), out_shape...  76.7 us
    pallas_call x1, Pallas kernels, on_device(): pl.pallas_call(functools.partial(correlate_kernel, scale), out_shape=jax....  5.93 us

profile of v3, /device:TPU:1, one launch (start us, length us, event | category | flops | bytes accessed | tf_op | source)
XLA Modules:
  0.0 82.6 jit_solution(15429841418421510334)
XLA Ops:
  0.0 76.7 %channelize_and_exchange.1 = (bf16[128,64,128]{2,1,0:T(8,128)(2,1)S(1)}, bf16[2,128,32,128]{3,2,1,0:T(8,128)(2,1)S(1)}, f32[2,4,512,512]{3,2,1,0:T(8,128)S(1)}) custom-call(s32[64,32768]{1,0:T(8,128)} %samples.1, s32[4,2048]{1,0:T(4,128)} %taps.1, bf16[2,128,16,2048]{3,2,1,0:T(8,128)(2,1)} %constant.2.clone.table), custom_call_target="tpu_custom_call" | custom-call | tf_op jit(solution)/shard_map/channelize_and_exchange/pallas_call | solution.py:351
  76.7 5.9 %correlate.1 = f32[2,8,512,512]{3,2,1,0:T(8,128)} custom-call(bf16[128,64,128]{2,1,0:T(8,128)(2,1)S(1)} %get-tuple-element.8.early, bf16[2,128,32,128]{3,2,1,0:T(8,128)(2,1)S(1)} %get-tuple-element.9.late, f32[2,4,512,512]{3,2,1,0:T(8,128)S(1)} %get-tuple-element.10.vis), custom_call_target="tpu_custom_call" | custom-call | tf_op jit(solution)/shard_map/correlate/pallas_call | solution.py:380

commit v4 on v3

--- a/solution.py
+++ b/solution.py
@@ -13,7 +13,8 @@
 LANES = 128
 QUAD = 4
 GROUP = 16
-STRIDE = 11
+STRIDE = 5
+AHEAD = 1
 PIECE = 32
 VMEM = 44 * 2**20
 
@@ -28,21 +29,18 @@
     high = rows.astype(ml_dtypes.bfloat16)
     low = (rows - high.astype(np.float64)).astype(ml_dtypes.bfloat16)
     parts = np.stack([high, low]).reshape(2, 2, devices, 2, QUAD, frame_len)
-    return parts.transpose(3, 2, 0, 1, 4, 5).reshape(2, devices, 4 * QUAD, frame_len)
-
-
-def peer(step, total):
+    return parts.transpose(3, 2, 0, 1, 4, 5).reshape(2, devices // 2, 2, 4 * QUAD, frame_len)
+
+
+def peer(step):
     inp, tm = lax.axis_index("inp"), lax.axis_index("tm")
-    plane = total // 4
-    rest = lax.max(step - plane, 0)
-    far = step >= plane
-    dz = jnp.where(far, 1 + lax.rem(rest, 3), 0)
-    mixed = lax.rem(jnp.where(far, lax.div(rest, 3), step) * STRIDE, plane)
-    x = lax.rem(lax.div(inp, 2) + lax.div(mixed, 8), 4)
-    y = lax.rem(lax.div(tm, 8) * 2 + lax.rem(inp, 2) + lax.rem(lax.div(mixed, 2), 4), 4)
-    z = lax.rem(lax.div(tm, 2) + dz, 4)
-    core = lax.rem(tm + mixed, 2)
-    return x * 2 + lax.rem(y, 2), lax.div(y, 2) * 8 + z * 2 + core
+    chip = lax.div(step, 2)
+    mixed = lax.rem(lax.div(chip, 4) * STRIDE, 16)
+    x = lax.rem(lax.div(inp, 2) + lax.div(mixed, 4), 4)
+    y = lax.rem(lax.div(tm, 8) * 2 + lax.rem(inp, 2) + mixed, 4)
+    z = lax.rem(lax.div(tm, 2) + chip, 4)
+    core = lax.rem(tm + step, 2)
+    return (x * 2 + lax.rem(y, 2), lax.div(y, 2) * 8 + z * 2 + core), chip * 2 + core
 
 
 def interleave(value):
@@ -115,6 +113,8 @@
     raw,
     past_out,
     past_in,
+    next_out,
+    next_in,
     filtered,
     tab,
     early_box,
@@ -122,6 +122,7 @@
     raw_sem,
     tab_sem,
     past_sem,
+    next_sem,
     send_sem,
     recv_sem,
     own_sem,
@@ -141,28 +142,35 @@
         cut = pl.ds(first * frame_len, count * frame_len)
         return pltpu.make_async_copy(samples.at[:, cut], raw.at[:, cut], raw_sem.at[part])
 
-    parts = [(spec_dev - back, back), (half - back, spec_dev - half), (0, half - back)]
-    for part, (first, count) in enumerate(parts[:2]):
+    before = back - AHEAD
+    quarter = spec_dev // 4
+    parts = [(spec_dev - before, before), (0, AHEAD)]
+    parts += [(quarter - before, half + back)]
+    parts += [(AHEAD, quarter - before - AHEAD), (quarter + half + AHEAD, quarter - AHEAD - before)]
+
+    def fetch(chip):
+        place, _ = peer(chip * 2)
+        pltpu.make_async_copy(
+            table.at[:, lax.div(place[0] * tm_count + place[1], 2)],
+            tab.at[:, pl.ds(chip * 2, 2)],
+            tab_sem.at[lax.div(chip * 2, GROUP)],
+        ).start()
+
+    def fetch_all(first, last):
+        def one(chip, carry):
+            fetch(chip)
+            return carry
+
+        lax.fori_loop(first, last, one, 0)
+
+    for part, (first, count) in enumerate(parts):
         load(part, first, count).start()
-
-    def fetch(group):
-        def one(k, carry):
-            step = group * GROUP + k
-            to_inp, to_tm = peer(step, total)
-            pltpu.make_async_copy(
-                table.at[:, to_inp * tm_count + to_tm], tab.at[:, step], tab_sem.at[group]
-            ).start()
-            return carry
-
-        lax.fori_loop(0, GROUP, one, 0)
-
-    fetch(0)
-    load(2, *parts[2]).start()
+    fetch_all(0, GROUP)
 
     barrier = pltpu.get_barrier_semaphore()
 
     def greet(step, carry):
-        pl.semaphore_signal(barrier, inc=1, device_id=peer(step, total), device_id_type=MESH)
+        pl.semaphore_signal(barrier, inc=1, device_id=peer(step)[0], device_id_type=MESH)
         return carry
 
     lax.fori_loop(1, total, greet, 0)
@@ -171,37 +179,39 @@
         taps[k : k + 1, cut].astype(jnp.float32) for k in range(tap_count)
     ]
 
-    def fir(first, count):
+    live = jnp.where(tm == tm_count - 1, 0.0, 1.0).astype(jnp.float32)
+
+    def fir(runs):
         def tile(n, carry):
             cut = pl.ds(pl.multiple_of(n * LANES, LANES), LANES)
             weights = weights_of(cut)
 
             def frame(s):
                 if s < 0:
-                    return past_in[(s + back) * inputs : (s + back + 1) * inputs, cut].astype(
-                        jnp.float32
-                    )
+                    at = (s + before) * inputs
+                    return past_in[at : at + inputs, cut].astype(jnp.float32)
+                if s >= spec_dev:
+                    return next_in[:, cut].astype(jnp.float32)
                 at = pl.ds(pl.multiple_of(s * frame_len + n * LANES, LANES), LANES)
                 return raw[:, at].astype(jnp.float32)
 
-            window = [frame(first - back + k) for k in range(back)]
-            for s in range(first, first + count):
-                window.append(frame(s))
-                value = weights[0] * window[0]
-                for k in range(1, tap_count):
-                    value = value + weights[k] * window[k]
-                filtered[s * inputs : (s + 1) * inputs, cut] = value.astype(jnp.bfloat16)
-                window.pop(0)
+            for first, count, row in runs:
+                window = [frame(first - before + k) for k in range(back)]
+                for s in range(first, first + count):
+                    window.append(frame(s + AHEAD))
+                    value = weights[0] * window[0]
+                    for k in range(1, back):
+                        value = value + weights[k] * window[k]
+                    if s + AHEAD == spec_dev:
+                        value = value * live
+                    value = value + weights[back] * window[back]
+                    at = row + (s - first) * inputs
+                    filtered[at : at + inputs, cut] = value.astype(jnp.bfloat16)
+                    window.pop(0)
             return carry
 
         lax.fori_loop(0, frame_len // LANES, tile, 0)
 
-    load(0, *parts[0]).wait()
-    for k in range(back):
-        first = (spec_dev - back + k) * frame_len
-        past_out[k * inputs : (k + 1) * inputs, :] = (
-            raw[:, first : first + frame_len].astype(jnp.float32).astype(jnp.bfloat16)
-        )
     def hand_on(piece):
         cut = pl.ds(piece * PIECE, PIECE)
         return pltpu.make_async_remote_copy(
@@ -213,31 +223,63 @@
             device_id_type=MESH,
         )
 
+    def hand_back(piece):
+        cut = pl.ds(piece * PIECE, PIECE)
+        return pltpu.make_async_remote_copy(
+            next_out.at[cut],
+            next_in.at[cut],
+            next_sem.at[0],
+            next_sem.at[1],
+            device_id=(inp, lax.rem(tm + tm_count - 1, tm_count)),
+            device_id_type=MESH,
+        )
+
+    load(0, *parts[0]).wait()
+    load(1, *parts[1]).wait()
+    for k in range(before):
+        first = (spec_dev - before + k) * frame_len
+        past_out[k * inputs : (k + 1) * inputs, :] = (
+            raw[:, first : first + frame_len].astype(jnp.float32).astype(jnp.bfloat16)
+        )
+    next_out[...] = raw[:, :frame_len].astype(jnp.float32).astype(jnp.bfloat16)
+
     pl.semaphore_wait(barrier, total - 1)
 
     @pl.when(tm < tm_count - 1)
     def _():
-        for piece in range(back * inputs // PIECE):
+        for piece in range(before * inputs // PIECE):
             hand_on(piece).start()
 
-    load(1, *parts[1]).wait()
-    fir(half, half)
+    for piece in range(AHEAD * inputs // PIECE):
+        hand_back(piece).start()
+
+    fetch_all(GROUP, total // 2)
+
+    load(2, *parts[2]).wait()
+    fir([(quarter, half, rows)])
+
+    def handed_over():
+        pltpu.make_async_copy(next_out, next_out, next_sem.at[0]).wait()
+
+        @pl.when(tm < tm_count - 1)
+        def _():
+            pltpu.make_async_copy(past_out, past_out, past_sem.at[0]).wait()
 
     boxes = [
-        (lambda step: early_box.at[step], lambda: early.at[me], early_box, early),
-        (lambda step: late_box.at[0, step], lambda: late.at[0, me], late_box.at[0], late.at[0]),
-        (lambda step: late_box.at[1, step], lambda: late.at[1, me], late_box.at[1], late.at[1]),
+        (lambda slot: early_box.at[slot], lambda: early.at[me], early_box, early),
+        (lambda slot: late_box.at[0, slot], lambda: late.at[0, me], late_box.at[0], late.at[0]),
+        (lambda slot: late_box.at[1, slot], lambda: late.at[1, me], late_box.at[1], late.at[1]),
     ]
 
     def own(phase):
         source, target = boxes[phase][:2]
-        return pltpu.make_async_copy(source(0), target(), own_sem.at[phase])
+        return pltpu.make_async_copy(source(peer(0)[1]), target(), own_sem.at[phase])
 
     def channelize(phase, base, halves):
         source, target = boxes[phase][:2]
 
         def group_step(index, carry):
-            group = index if phase == 0 else lax.rem(index * 3 + 2, groups)
+            group = index
             at = pl.ds(group * GROUP, GROUP)
             if phase == 0:
 
@@ -256,8 +298,12 @@
                 else:
                     late_box[h, at] = box
 
+            if phase == 0:
+                pl.when(index == 0)(handed_over)
+
             def send(k, carry):
                 step = group * GROUP + k
+                place, slot = peer(step)
 
                 @pl.when(step == 0)
                 def _():
@@ -266,11 +312,11 @@
                 @pl.when(step > 0)
                 def _():
                     pltpu.make_async_remote_copy(
-                        source(step),
+                        source(slot),
                         target(),
                         send_sem.at[phase],
                         recv_sem.at[phase],
-                        device_id=peer(step, total),
+                        device_id=place,
                         device_id_type=MESH,
                     ).start()
 
@@ -281,8 +327,6 @@
 
         lax.fori_loop(0, groups, group_step, 0)
 
-    for g in range(1, groups):
-        fetch(g)
     channelize(0, rows, (0, 1))
 
     @pl.when(tm > 0)
@@ -293,8 +337,10 @@
     def _():
         past_in[...] = jnp.zeros_like(past_in)
 
-    load(2, *parts[2]).wait()
-    fir(0, half)
+    pltpu.make_async_copy(next_in, next_in, next_sem.at[1]).wait()
+    load(3, *parts[3]).wait()
+    load(4, *parts[4]).wait()
+    fir([(0, quarter, 0), (quarter + half, quarter, quarter * inputs)])
     channelize(1, 0, (0,))
     channelize(2, 0, (1,))
 
@@ -312,10 +358,6 @@
     for phase in range(3):
         sent = boxes[phase][2].at[others]
         pltpu.make_async_copy(sent, sent, send_sem.at[phase]).wait()
-
-    @pl.when(tm < tm_count - 1)
-    def _():
-        pltpu.make_async_copy(past_out, past_out, past_sem.at[0]).wait()
 
 
 def correlate_kernel(scale, early, late, vis, out, rest, sem):
@@ -359,14 +401,17 @@
         out_specs=[vmem, vmem, vmem],
         scratch_shapes=[
             pltpu.VMEM(samples.shape, jnp.int32),
-            pltpu.VMEM(((tap_count - 1) * inputs, frame_len), bf16),
-            pltpu.VMEM(((tap_count - 1) * inputs, frame_len), bf16),
+            pltpu.VMEM(((tap_count - 1 - AHEAD) * inputs, frame_len), bf16),
+            pltpu.VMEM(((tap_count - 1 - AHEAD) * inputs, frame_len), bf16),
+            pltpu.VMEM((AHEAD * inputs, frame_len), bf16),
+            pltpu.VMEM((AHEAD * inputs, frame_len), bf16),
             pltpu.VMEM((spec_dev * inputs, frame_len), bf16),
             pltpu.VMEM((2, total, 4 * QUAD, frame_len), bf16),
             pltpu.VMEM(early_shape, bf16),
             pltpu.VMEM(late_shape, bf16),
-            pltpu.SemaphoreType.DMA((3,)),
+            pltpu.SemaphoreType.DMA((5,)),
             pltpu.SemaphoreType.DMA((groups,)),
+            pltpu.SemaphoreType.DMA((2,)),
             pltpu.SemaphoreType.DMA((2,)),
             pltpu.SemaphoreType.DMA((3,)),
             pltpu.SemaphoreType.DMA((3,)),

time: 82.8 us -> 78.5 us (0.948)
  Pallas kernels: 82.6 us -> 78.3 us
    pallas_call x1, Pallas kernels: 76.7 us -> 72.4 us  [on_device(): pl.pallas_call(functools.partial(spectra_kernel, total, scale), out_shape...]
where the time goes in v4:
time: 78.5 us; the launch traced here: 78.3 us
  Pallas kernels  78.3 us (100%)
    pallas_call x1, Pallas kernels, on_device(): pl.pallas_call(functools.partial(spectra_kernel, total, scale), out_shape...  72.4 us
    pallas_call x1, Pallas kernels, on_device(): pl.pallas_call(functools.partial(correlate_kernel, scale), out_shape=jax....  5.93 us

profile of v4, /device:TPU:1, one launch (start us, length us, event | category | flops | bytes accessed | tf_op | source)
XLA Modules:
  0.0 78.3 jit_solution(7794325220787898337)
XLA Ops:
  0.0 72.4 %channelize_and_exchange.1 = (bf16[128,64,128]{2,1,0:T(8,128)(2,1)S(1)}, bf16[2,128,32,128]{3,2,1,0:T(8,128)(2,1)S(1)}, f32[2,4,512,512]{3,2,1,0:T(8,128)S(1)}) custom-call(s32[64,32768]{1,0:T(8,128)} %samples.1, s32[4,2048]{1,0:T(4,128)} %taps.1, bf16[2,64,2,16,2048]{4,3,2,1,0:T(8,128)(2,1)} %constant.2.clone.table), custom_call_target="tpu_custom_call" | custom-call | tf_op jit(solution)/shard_map/channelize_and_exchange/pallas_call | solution.py:393
  72.4 5.9 %correlate.1 = f32[2,8,512,512]{3,2,1,0:T(8,128)} custom-call(bf16[128,64,128]{2,1,0:T(8,128)(2,1)S(1)} %get-tuple-element.8.early, bf16[2,128,32,128]{3,2,1,0:T(8,128)(2,1)S(1)} %get-tuple-element.9.late, f32[2,4,512,512]{3,2,1,0:T(8,128)S(1)} %get-tuple-element.10.vis), custom_call_target="tpu_custom_call" | custom-call | tf_op jit(solution)/shard_map/correlate/pallas_call | solution.py:425

commit v5 on v4

--- a/solution.py
+++ b/solution.py
@@ -13,7 +13,7 @@
 LANES = 128
 QUAD = 4
 GROUP = 16
-STRIDE = 5
+STRIDE = 11
 AHEAD = 1
 PIECE = 32
 VMEM = 44 * 2**20
@@ -32,13 +32,13 @@
     return parts.transpose(3, 2, 0, 1, 4, 5).reshape(2, devices // 2, 2, 4 * QUAD, frame_len)
 
 
-def peer(step):
+def peer(group, step):
     inp, tm = lax.axis_index("inp"), lax.axis_index("tm")
-    chip = lax.div(step, 2)
-    mixed = lax.rem(lax.div(chip, 4) * STRIDE, 16)
+    chip = group * (GROUP // 2) + lax.div(step, 2)
+    mixed = lax.rem((group * (GROUP // 8) + lax.div(step, 8)) * STRIDE, 16)
     x = lax.rem(lax.div(inp, 2) + lax.div(mixed, 4), 4)
     y = lax.rem(lax.div(tm, 8) * 2 + lax.rem(inp, 2) + mixed, 4)
-    z = lax.rem(lax.div(tm, 2) + chip, 4)
+    z = lax.rem(lax.div(tm, 2) + lax.div(step, 2), 4)
     core = lax.rem(tm + step, 2)
     return (x * 2 + lax.rem(y, 2), lax.div(y, 2) * 8 + z * 2 + core), chip * 2 + core
 
@@ -149,7 +149,7 @@
     parts += [(AHEAD, quarter - before - AHEAD), (quarter + half + AHEAD, quarter - AHEAD - before)]
 
     def fetch(chip):
-        place, _ = peer(chip * 2)
+        place, _ = peer(0, chip * 2)
         pltpu.make_async_copy(
             table.at[:, lax.div(place[0] * tm_count + place[1], 2)],
             tab.at[:, pl.ds(chip * 2, 2)],
@@ -163,17 +163,20 @@
 
         lax.fori_loop(first, last, one, 0)
 
-    for part, (first, count) in enumerate(parts):
-        load(part, first, count).start()
-    fetch_all(0, GROUP)
-
+    def load_all(first, last):
+        for part in range(first, last):
+            load(part, *parts[part]).start()
+
+    load_all(0, 2)
     barrier = pltpu.get_barrier_semaphore()
 
-    def greet(step, carry):
-        pl.semaphore_signal(barrier, inc=1, device_id=peer(step)[0], device_id_type=MESH)
-        return carry
-
-    lax.fori_loop(1, total, greet, 0)
+    def greet(group, first):
+        for k in range(first, GROUP):
+            pl.semaphore_signal(barrier, inc=1, device_id=peer(group, k)[0], device_id_type=MESH)
+        return 0
+
+    for group in range(groups):
+        greet(group, 1 if group == 0 else 0)
 
     weights_of = lambda cut: [
         taps[k : k + 1, cut].astype(jnp.float32) for k in range(tap_count)
@@ -234,6 +237,9 @@
             device_id_type=MESH,
         )
 
+    load_all(2, 3)
+    fetch_all(0, GROUP // 2)
+    load_all(3, 5)
     load(0, *parts[0]).wait()
     load(1, *parts[1]).wait()
     for k in range(before):
@@ -253,7 +259,7 @@
     for piece in range(AHEAD * inputs // PIECE):
         hand_back(piece).start()
 
-    fetch_all(GROUP, total // 2)
+    fetch_all(GROUP // 2, total // 2)
 
     load(2, *parts[2]).wait()
     fir([(quarter, half, rows)])
@@ -273,7 +279,7 @@
 
     def own(phase):
         source, target = boxes[phase][:2]
-        return pltpu.make_async_copy(source(peer(0)[1]), target(), own_sem.at[phase])
+        return pltpu.make_async_copy(source(peer(0, 0)[1]), target(), own_sem.at[phase])
 
     def channelize(phase, base, halves):
         source, target = boxes[phase][:2]
@@ -301,28 +307,26 @@
             if phase == 0:
                 pl.when(index == 0)(handed_over)
 
-            def send(k, carry):
-                step = group * GROUP + k
-                place, slot = peer(step)
-
-                @pl.when(step == 0)
-                def _():
-                    own(phase).start()
-
-                @pl.when(step > 0)
-                def _():
-                    pltpu.make_async_remote_copy(
-                        source(slot),
-                        target(),
-                        send_sem.at[phase],
-                        recv_sem.at[phase],
-                        device_id=place,
-                        device_id_type=MESH,
-                    ).start()
-
-                return carry
-
-            lax.fori_loop(0, GROUP, send, 0)
+            def send(place, slot):
+                pltpu.make_async_remote_copy(
+                    source(slot),
+                    target(),
+                    send_sem.at[phase],
+                    recv_sem.at[phase],
+                    device_id=place,
+                    device_id_type=MESH,
+                ).start()
+
+            @pl.when(index == 0)
+            def _():
+                own(phase).start()
+
+            @pl.when(index > 0)
+            def _():
+                send(*peer(group, 0))
+
+            for k in range(1, GROUP):
+                send(*peer(group, k))
             return carry
 
         lax.fori_loop(0, groups, group_step, 0)

time: 78.5 us -> 71.9 us (0.916)
  Pallas kernels: 78.3 us -> 71.6 us
    pallas_call x1, Pallas kernels: 72.4 us -> 65.6 us  [on_device(): pl.pallas_call(functools.partial(spectra_kernel, total, scale), out_shape...]
where the time goes in v5:
time: 71.9 us; the launch traced here: 71.6 us
  Pallas kernels  71.6 us (100%)
    pallas_call x1, Pallas kernels, on_device(): pl.pallas_call(functools.partial(spectra_kernel, total, scale), out_shape...  65.6 us
    pallas_call x1, Pallas kernels, on_device(): pl.pallas_call(functools.partial(correlate_kernel, scale), out_shape=jax....  5.93 us

profile of v5, /device:TPU:1, one launch (start us, length us, event | category | flops | bytes accessed | tf_op | source)
XLA Modules:
  0.0 71.6 jit_solution(5951908946503283863)
XLA Ops:
  0.0 65.6 %channelize_and_exchange.1 = (bf16[128,64,128]{2,1,0:T(8,128)(2,1)S(1)}, bf16[2,128,32,128]{3,2,1,0:T(8,128)(2,1)S(1)}, f32[2,4,512,512]{3,2,1,0:T(8,128)S(1)}) custom-call(s32[64,32768]{1,0:T(8,128)} %samples.1, s32[4,2048]{1,0:T(4,128)} %taps.1, bf16[2,64,2,16,2048]{4,3,2,1,0:T(8,128)(2,1)} %constant.2.clone.table), custom_call_target="tpu_custom_call" | custom-call | tf_op jit(solution)/shard_map/channelize_and_exchange/pallas_call | solution.py:397
  65.6 5.9 %correlate.1 = f32[2,8,512,512]{3,2,1,0:T(8,128)} custom-call(bf16[128,64,128]{2,1,0:T(8,128)(2,1)S(1)} %get-tuple-element.8.early, bf16[2,128,32,128]{3,2,1,0:T(8,128)(2,1)S(1)} %get-tuple-element.9.late, f32[2,4,512,512]{3,2,1,0:T(8,128)S(1)} %get-tuple-element.10.vis), custom_call_target="tpu_custom_call" | custom-call | tf_op jit(solution)/shard_map/correlate/pallas_call | solution.py:429

commit v6 on v5

--- a/solution.py
+++ b/solution.py
@@ -13,7 +13,7 @@
 LANES = 128
 QUAD = 4
 GROUP = 16
-STRIDE = 11
+STRIDE = 9
 AHEAD = 1
 PIECE = 32
 VMEM = 44 * 2**20

time: 71.9 us -> 72 us (level)
  no operation moved by 1% of the time
where the time goes in v6:
time: 72 us; the launch traced here: 71.8 us
  Pallas kernels  71.8 us (100%)
    pallas_call x1, Pallas kernels, on_device(): pl.pallas_call(functools.partial(spectra_kernel, total, scale), out_shape...  65.9 us
    pallas_call x1, Pallas kernels, on_device(): pl.pallas_call(functools.partial(correlate_kernel, scale), out_shape=jax....  5.93 us

profile of v6, /device:TPU:1, one launch (start us, length us, event | category | flops | bytes accessed | tf_op | source)
XLA Modules:
  0.0 71.8 jit_solution(10263450653653647867)
XLA Ops:
  0.0 65.9 %channelize_and_exchange.1 = (bf16[128,64,128]{2,1,0:T(8,128)(2,1)S(1)}, bf16[2,128,32,128]{3,2,1,0:T(8,128)(2,1)S(1)}, f32[2,4,512,512]{3,2,1,0:T(8,128)S(1)}) custom-call(s32[64,32768]{1,0:T(8,128)} %samples.1, s32[4,2048]{1,0:T(4,128)} %taps.1, bf16[2,64,2,16,2048]{4,3,2,1,0:T(8,128)(2,1)} %constant.2.clone.table), custom_call_target="tpu_custom_call" | custom-call | tf_op jit(solution)/shard_map/channelize_and_exchange/pallas_call | solution.py:397
  65.9 5.9 %correlate.1 = f32[2,8,512,512]{3,2,1,0:T(8,128)} custom-call(bf16[128,64,128]{2,1,0:T(8,128)(2,1)S(1)} %get-tuple-element.8.early, bf16[2,128,32,128]{3,2,1,0:T(8,128)(2,1)S(1)} %get-tuple-element.9.late, f32[2,4,512,512]{3,2,1,0:T(8,128)S(1)} %get-tuple-element.10.vis), custom_call_target="tpu_custom_call" | custom-call | tf_op jit(solution)/shard_map/correlate/pallas_call | solution.py:429
